TPU v7x, 32 devices: a whole 2x2x4 slice. The times are simulated.
32 devices in a mesh: rep: 2 (over y), row: 4 (over x, core), col: 4 (over z).
Axes of the slice: x: 2, y: 2, z: 4, core: 2. Of those that a mesh axis runs over, the one named last changes fastest.
Arguments:
- density: bfloat16 [8192, 4096], P(('rep', 'col'), 'row'), parts along dimension 0, may hold values from -2.5 to 2.5
- pattern: int32 [32, 16], P('rep'), parts along dimension 0, may hold values from 0 to 1, as said below
Outputs:
- product: float32 [8192, 4096], P(('rep', 'col'), 'row'), parts along dimension 0
There are 2 independent parts, one for each index of `rep`. A program takes and returns all parts, laid end to end along the dimension named above; each array names one. Nothing has to cross between parts.
Inputs may be any that keep to these rules, and one draw needn't show every extreme that they name: `pattern`: block (a, b) is filled where b = a or b = (a + 1) mod 16. In each block row, at most 2 filled blocks lie in any aligned group of 4 block columns, and some block row reaches that bound. Block rows differ in how many blocks are filled.
All inputs are finite; a program needn't handle non-finite values.
Results may differ from a plain program's by a relative error of at most 0.0003.
Values may be sent and summed in bfloat16 or wider, within the bound.
A program may use at most 64 MiB of HBM per device.

v0:
```python
import jax
import jax.numpy as jnp
from jax import lax
from jax.sharding import PartitionSpec as P

BLK = 256


def broadcast(value, axis, source):
    kept = jnp.where(lax.axis_index(axis) == source, value, 0).astype(value.dtype)
    return lax.psum(kept, axis)


def from_behind(array, axis, by):
    count = lax.axis_size(axis)
    return lax.ppermute(array, axis, [(i, (i + by) % count) for i in range(count)])


def expand_mask(blocks, size_blk):
    count_r, count_c = blocks.shape
    full_mask = jnp.broadcast_to(blocks[:, None, :, None], (count_r, size_blk, count_c, size_blk))
    return full_mask.reshape(count_r * size_blk, count_c * size_blk)


def multiply(left, right):
    return jnp.dot(left, right, preferred_element_type=jnp.float32)


def local(density, pattern):
    stripe, width = density.shape
    size_blk = BLK
    count_col = lax.axis_size("col")
    count_row = lax.axis_size("row")
    ratio = count_col // count_row
    stripe_idx = lax.axis_index("col")
    column_idx = lax.axis_index("row")
    nblk_r = stripe // size_blk
    nblk_c = width // size_blk
    own_blocks = lax.dynamic_slice(
        pattern, (stripe_idx * nblk_r, column_idx * nblk_c), (nblk_r, nblk_c)
    )
    masked = density * expand_mask(own_blocks, size_blk).astype(jnp.bfloat16)
    tiles = masked.reshape(stripe, ratio, stripe)

    def section_tile(section):
        other = (stripe_idx + section) % count_col
        mine = lax.dynamic_index_in_dim(tiles, other % ratio, 1, keepdims=False)
        return broadcast(mine, "row", other // ratio)

    first_tile = section_tile(0)
    second_tile = section_tile(1)
    first_term = multiply(first_tile, masked)
    panel = from_behind(masked, "col", -1)
    second_term = multiply(second_tile, panel)
    return first_term + second_term


def solution(mesh):
    placed = (P(("rep", "col"), "row"), P("rep", None))
    return jax.shard_map(
        local, mesh=mesh, in_specs=placed, out_specs=P(("rep", "col"), "row"), check_vma=False
    )
```

profile of v0, /device:TPU:0, one launch (start us, length us, event | category | flops | bytes accessed | tf_op | source)
XLA Modules:
  0.0 118.0 jit_solution(17158950515743482495)
XLA Ops:
  6.5 0.0 all-reduce.3.cloned.1.call-start
  6.5 0.8 dynamic-slice_convert_fusion
  7.3 0.6 broadcast_in_dim.11
  7.9 0.0 copy-start
  7.9 0.5 copy.3
  8.4 1.1 copy-done
  9.5 1.6 %broadcast_select_fusion = (bf16[1024,1024]{1,0:T(8,128)(2,1)}, bf16[1024,1024]{1,0:T(8,128)(2,1)S(1)}) fusion(pred[]{:T(512)S(6)} %eq.12, bf16[1024,1024]{1,0:T(8,128)(2,1)S(1)} %copy-done, bf16[1024,1024]{1,0:T(8,128)(2,1)S(1)} %bitcast.8), kind=kLoop, calls=%fused_computation | loop fusion | flops 2097152 | bytes 8388609 | tf_op jit(solution)/shard_map/jit(_where)/select_n | solution.py:10
  11.1 1.5 %broadcast_select_fusion.1 = bf16[1024,1024]{1,0:T(8,128)(2,1)} fusion(bf16[1024,1024]{1,0:T(8,128)(2,1)S(1)} %get-tuple-element.8, pred[]{:T(512)S(6)} %eq.11), kind=kLoop, calls=%fused_computation.1 | loop fusion | flops 1048576 | bytes 4194305 | tf_op jit(solution)/shard_map/jit(_where)/select_n | solution.py:10
  12.6 0.0 all-reduce.3.cloned.1.call-update
  12.6 5.1 %collective-permute-start = (bf16[1024,1024]{1,0:T(8,128)(2,1)S(1)}, bf16[1024,1024]{1,0:T(8,128)(2,1)}, u32[]{:S(2)}, u32[]{:S(2)}) collective-permute-start(bf16[1024,1024]{1,0:T(8,128)(2,1)S(1)} %get-tuple-element.8), channel_id=1, source_target_pairs={{0,3},{1,0},{2,1},{3,2},{4,7},{5,4},{6,5},{7,6},{8,11},{9,8},{10,9... | collective-permute-start | bytes 6291464 | tf_op jit(solution)/shard_map/ppermute | solution.py:16
  17.7 83.4 %all-reduce.3.cloned.1.call-done = (bf16[1024,1024]{1,0:T(8,128)(2,1)}, bf16[1024,1024]{1,0:T(8,128)(2,1)}) async-done(((bf16[1024,1024]{1,0:T(8,128)(2,1)}, bf16[1024,1024]{1,0:T(8,128)(2,1)}), (bf16[1024,1024]{1,0:T(8,128)(2,1)}, bf16[1024,1024]{1,0:T(8,128)(2,1)})) %all-reduce.3.cloned.1.call-update) | async-done | bytes 4194320 | tf_op jit(solution)/shard_map/psum | solution.py:11
  101.1 0.0 copy-start.1
  101.1 4.1 %fusion = f32[1024,1024]{1,0:T(8,128)S(1)} fusion(bf16[1024,1024]{1,0:T(8,128)(2,1)} %get-tuple-element.5, bf16[1024,1024]{1,0:T(8,128)(2,1)S(1)} %get-tuple-element.8), kind=kOutput, calls=%fused_computation.4 | convolution fusion | flops 2147483648 | bytes 8388608 | tf_op jit(solution)/shard_map/dot_general | solution.py:26
  105.2 0.0 collective-permute-done
  105.2 0.0 copy-done.1
  105.2 6.0 %convolution_add_fusion = f32[1024,1024]{1,0:T(8,128)} fusion(f32[1024,1024]{1,0:T(8,128)S(1)} %fusion, bf16[1024,1024]{1,0:T(8,128)(2,1)S(1)} %copy-done.1, bf16[1024,1024]{1,0:T(8,128)(2,1)} %collective-permute-done), kind=kOutput, calls=%fused_computation.2 | convolution fusion | flops 2148532224 | bytes 12582912 | tf_op jit(solution)/shard_map/dot_general | solution.py:26
Async XLA Ops:
  6.5 94.6 %all-reduce.3.cloned.1.call-start = ((), (), s32[]{:S(2)}) async-start(), calls=%async_computation | async-start | bytes 8388608 | tf_op jit(solution)/shard_map/psum | solution.py:11
  7.9 1.6 %copy-start = (bf16[1024,1024]{1,0:T(8,128)(2,1)S(1)}, bf16[1024,1024]{1,0:T(8,128)(2,1)}, u32[]{:S(2)}) copy-start(bf16[1024,1024]{1,0:T(8,128)(2,1)} %param.2) | copy-start | bytes 6291460
  12.6 92.6 %collective-permute-start = (bf16[1024,1024]{1,0:T(8,128)(2,1)S(1)}, bf16[1024,1024]{1,0:T(8,128)(2,1)}, u32[]{:S(2)}, u32[]{:S(2)}) collective-permute-start(bf16[1024,1024]{1,0:T(8,128)(2,1)S(1)} %get-tuple-element.8), channel_id=1, source_target_pairs={{0,3},{1,0},{2,1},{3,2},{4,7},{5,4},{6,5},{7,6},{8,11},{9,8},{10,9... | collective-permute-start | bytes 6291464 | tf_op jit(solution)/shard_map/ppermute | solution.py:16
  101.1 4.1 %copy-start.1 = (bf16[1024,1024]{1,0:T(8,128)(2,1)S(1)}, bf16[1024,1024]{1,0:T(8,128)(2,1)}, u32[]{:S(2)}) copy-start(bf16[1024,1024]{1,0:T(8,128)(2,1)} %get-tuple-element.6) | copy-start | bytes 6291460
Sparse Core Ops, SparseCore 0:
  12.7 88.3 all-reduce.2
where the time goes:
time: 118 us
  waiting for transfers between devices  83.4 us (71%)
  between operations  13.4 us (11%)
  matrix products  10 us (8%)
  starting transfers between devices  5.1 us (4%)
  other arithmetic  3.8 us (3%)
  local copies, waits for them, and re-layouts  2.19 us (2%)
    psum x1, waiting for transfers between devices, broadcast(): return lax.psum(kept, axis)  83.4 us
    dot_general x2, matrix products, multiply(): return jnp.dot(left, right, preferred_element_type=jnp.float32)  10 us
    ppermute x1, starting transfers between devices, from_behind(): lax.ppermute(array, axis, [(i, (i + by) % count) for i in range(count)])  5.1 us
    select_n x2, other arithmetic, broadcast(): jnp.where(lax.axis_index(axis) == source, value, 0).astype(value.dtype)  3.04 us
  transfers between devices with their start and end apart: 2, of which 1 were waited for; matrix products, arithmetic and copies ran while one was open for 3% of the time, Pallas kernels for 0%

commit v1 on v0

v1 whole, which is shorter than its diff:
```python
import functools

import jax
import jax.numpy as jnp
from jax import lax
from jax.experimental import pallas as pl
from jax.experimental.pallas import tpu as pltpu
from jax.sharding import PartitionSpec as P

BLK = 256
SLOTS = 2
CORES = 2


def kernel(sizes, pat, dens, out, own, tile_a, tile_b, lhs, *rest):
    rows, cols, n_row, n_col = sizes
    panels, rest = rest[:rows], rest[rows:]
    raw, rest = rest[:rows], rest[rows:]
    raw_sem, z_send, z_recv, x_send, x_recv, fwd_send, keep_sem = rest
    tiles = (tile_a, tile_b)
    zero_at = rows * SLOTS
    chips = n_row // CORES
    ratio = cols // rows

    row, col = lax.axis_index("row"), lax.axis_index("col")
    chip, core = row // CORES, row % CORES
    sibling = chip * CORES + (CORES - 1 - core)
    below, above = (col + n_col - 1) % n_col, (col + 1) % n_col
    wanted = (col, above)
    source = [w // ratio for w in wanted]
    shift = [(w % ratio) * rows for w in wanted]

    barrier = pltpu.get_barrier_semaphore()
    for step in range(1, n_row):
        pl.semaphore_signal(barrier, inc=1, device_id={"row": (row + step) % n_row})
    pl.semaphore_signal(barrier, inc=1, device_id={"col": below})
    pl.semaphore_signal(barrier, inc=1, device_id={"col": above})

    def fetch(r):
        return pltpu.make_async_copy(dens.at[pl.ds(r * BLK, BLK)], raw[r], raw_sem.at[r])

    for r in range(rows):
        fetch(r).start()

    def column_of(block_row, device, slot):
        count, column, found = 0, 0, 0
        for c in range(cols):
            here = pat[block_row, device * cols + c]
            hit = jnp.where(count == slot, here, 0)
            column = column + hit * c
            found = found + hit
            count = count + here
        return column, found

    def slot_of(block_row, device, column):
        count, here = 0, 0
        for c in range(cols):
            value = pat[block_row, device * cols + c]
            count = count + jnp.where(c < column, value, 0)
            here = here + jnp.where(c == column, value, 0)
        return jnp.where(here == 0, -1, jnp.minimum(count, SLOTS - 1))

    def piece(ref, r):
        return ref.at[pl.ds(r * SLOTS, SLOTS)]

    def down(r):
        return pltpu.make_async_remote_copy(
            piece(own, r), panels[r].at[pl.ds(0, SLOTS)], z_send.at[r], z_recv.at[r],
            device_id={"col": below},
        )

    def spread(t, r, j):
        target = sibling if j == 0 else ((chip + j) % chips) * CORES + core
        return pltpu.make_async_remote_copy(
            piece(own, r), piece(tiles[t], r), x_send.at[t, r, j], x_recv.at[t, r],
            device_id={"row": target},
        )

    def forward(t, r):
        return pltpu.make_async_remote_copy(
            piece(tiles[t], r), piece(tiles[t], r), fwd_send.at[t, r], x_recv.at[t, r],
            device_id={"row": sibling},
        )

    def keep(t, r):
        return pltpu.make_async_copy(piece(own, r), piece(tiles[t], r), keep_sem.at[t, r])

    zero = jnp.zeros((BLK, BLK), own.dtype)
    for r in range(rows):
        fetch(r).wait()
        for s in range(SLOTS):
            block = None
            for c in range(cols):
                hit = (slot_of(col * rows + r, row, c) == s).astype(jnp.int32)
                term = raw[r][:, c * BLK : (c + 1) * BLK] * hit.astype(own.dtype)
                block = term if block is None else block + term
            own[r * SLOTS + s] = block
        if r == 0:
            pl.semaphore_wait(barrier, n_row + 1)
        down(r).start()
        for t in range(2):
            @pl.when(row == source[t])
            def _():
                for j in reversed(range(chips)):
                    spread(t, r, j).start()
                keep(t, r).start()

    own[zero_at] = zero
    tile_b[zero_at] = zero
    for r in range(rows):
        panels[r][SLOTS] = zero

    held = []
    for k in range(rows):
        slots = [slot_of(col * rows + k, row, c) for c in range(cols)]
        held.append([jnp.where(slot >= 0, k * SLOTS + slot, zero_at) for slot in slots])

    relays = [(chip != source[t] // CORES) & (core == source[t] % CORES) for t in range(2)]
    for r in range(rows):
        for t in range(2):
            @pl.when(row == source[t])
            def _():
                keep(t, r).wait()

            @pl.when(row != source[t])
            def _():
                spread(t, r, 0).wait_recv()

            @pl.when(relays[t])
            def _():
                forward(t, r).start()

        for c in range(cols):
            total = None
            for s in range(SLOTS):
                column, found = column_of(col * rows + r, source[0], s)
                at = zero_at
                for k in range(rows):
                    here = (found != 0) & (column == shift[0] + k)
                    at = jnp.where(here, held[k][c], at)
                term = jnp.dot(
                    tile_a[r * SLOTS + s], own[at], preferred_element_type=jnp.float32
                )
                total = term if total is None else total + term
            out[pl.ds(r * BLK, BLK), pl.ds(c * BLK, BLK)] = total

    for k in range(rows):
        for r in range(rows):
            slot = slot_of(col * rows + r, source[1], shift[1] + k)
            at = jnp.where(slot >= 0, r * SLOTS + slot, zero_at)
            lhs[pl.ds(r * BLK, BLK), :] = tile_b[at]
        down(k).wait_recv()

        def second_term(c, carry):
            slot = slot_of(above * rows + k, row, c)
            at = jnp.where(slot >= 0, slot, SLOTS)
            where = pl.ds(pl.multiple_of(c * BLK, BLK), BLK)
            out[:, where] += jnp.dot(
                lhs[...], panels[k][at], preferred_element_type=jnp.float32
            )
            return carry

        lax.fori_loop(0, cols, second_term, 0)

    for r in range(rows):
        down(r).wait_send()
        for t in range(2):
            @pl.when(row == source[t])
            def _():
                for j in range(chips):
                    spread(t, r, j).wait_send()

            @pl.when(relays[t])
            def _():
                forward(t, r).wait_send()


def local(density, pattern):
    stripe, width = density.shape
    rows, cols = stripe // BLK, width // BLK
    n_row, n_col = lax.axis_size("row"), lax.axis_size("col")
    chips = n_row // CORES
    dtype = density.dtype
    packed = pltpu.VMEM((rows * SLOTS + 1, BLK, BLK), dtype)
    return pl.pallas_call(
        functools.partial(kernel, (rows, cols, n_row, n_col)),
        out_shape=jax.ShapeDtypeStruct((stripe, width), jnp.float32),
        in_specs=[
            pl.BlockSpec(memory_space=pltpu.SMEM),
            pl.BlockSpec(memory_space=pl.ANY),
        ],
        out_specs=pl.BlockSpec(memory_space=pltpu.VMEM),
        scratch_shapes=[packed] * 3
        + [pltpu.VMEM((stripe, BLK), dtype)]
        + [pltpu.VMEM((SLOTS + 1, BLK, BLK), dtype)] * rows
        + [pltpu.VMEM((BLK, width), dtype)] * rows
        + [
            pltpu.SemaphoreType.DMA((rows,)),
            pltpu.SemaphoreType.DMA((rows,)),
            pltpu.SemaphoreType.DMA((rows,)),
            pltpu.SemaphoreType.DMA((2, rows, chips)),
            pltpu.SemaphoreType.DMA((2, rows)),
            pltpu.SemaphoreType.DMA((2, rows)),
            pltpu.SemaphoreType.DMA((2, rows)),
        ],
        compiler_params=pltpu.CompilerParams(
            collective_id=0, has_side_effects=True, vmem_limit_bytes=40 * 1024 * 1024
        ),
        cost_estimate=pl.CostEstimate(
            flops=4 * stripe * stripe * width,
            bytes_accessed=6 * stripe * width,
            transcendentals=0,
        ),
    )(pattern, density)


def solution(mesh):
    placed = (P(("rep", "col"), "row"), P("rep", None))
    return jax.shard_map(
        local, mesh=mesh, in_specs=placed, out_specs=P(("rep", "col"), "row"), check_vma=False
    )
```

time: 118 us -> 40.9 us (0.35)
  the two profiles are of different devices: /device:TPU:0 before, /device:TPU:2 now
where the time goes in v1:
time: 40.9 us; the launch traced here: 40.7 us
  Pallas kernels  36.4 us (89%)
  local copies, waits for them, and re-layouts  4.3 us (11%)
    pallas_call x1, Pallas kernels, local(): pl.pallas_call(functools.partial(kernel, (rows, cols, n_row, n_col)), out...  36.4 us
    unnamed x5, local copies, waits for them, and re-layouts  4.3 us

profile of v1, /device:TPU:2, one launch (start us, length us, event | category | flops | bytes accessed | tf_op | source)
XLA Modules:
  0.0 40.7 jit_solution(5215788984270541922)
XLA Ops:
  0.0 0.0 copy-start
  0.0 1.6 %copy-done = bf16[1024,1024]{1,0:T(8,128)(2,1)S(1)} copy-done((bf16[1024,1024]{1,0:T(8,128)(2,1)S(1)}, bf16[1024,1024]{1,0:T(8,128)(2,1)}, u32[]{:S(2)}) %copy-start) | copy-done | bytes 2097176
  1.6 0.0 copy-start.1
  1.6 0.7 %copy-done.1 = s32[16,16]{1,0:T(8,128)S(1)} copy-done((s32[16,16]{1,0:T(8,128)S(1)}, s32[16,16]{1,0:T(8,128)}, u32[]{:S(2)}) %copy-start.1) | copy-done | bytes 1048
  2.3 36.4 %shard_map.28 = f32[1024,1024]{1,0:T(8,128)S(1)} custom-call(s32[16,16]{1,0:T(8,128)S(1)} %copy-done.1, bf16[1024,1024]{1,0:T(8,128)(2,1)S(1)} %copy-done), custom_call_target="tpu_custom_call" | custom-call | flops 4294967296 | bytes 6291456 | tf_op jit(solution)/shard_map/pallas_call | solution.py:185
  38.7 2.0 %copy.4 = f32[1024,1024]{1,0:T(8,128)} copy(f32[1024,1024]{1,0:T(8,128)S(1)} %shard_map.28) | data formatting | bytes 8388608
Async XLA Ops:
  0.0 1.6 %copy-start = (bf16[1024,1024]{1,0:T(8,128)(2,1)S(1)}, bf16[1024,1024]{1,0:T(8,128)(2,1)}, u32[]{:S(2)}) copy-start(bf16[1024,1024]{1,0:T(8,128)(2,1)} %dens.1) | copy-start | bytes 6291460
  1.6 0.7 %copy-start.1 = (s32[16,16]{1,0:T(8,128)S(1)}, s32[16,16]{1,0:T(8,128)}, u32[]{:S(2)}) copy-start(s32[16,16]{1,0:T(8,128)} %pat.1) | copy-start | bytes 3076

commit v2 on v1

--- a/solution.py
+++ b/solution.py
@@ -12,11 +12,11 @@
 CORES = 2
 
 
-def kernel(sizes, pat, dens, out, own, tile_a, tile_b, lhs, *rest):
+def kernel(sizes, pat_hbm, dens, out, pat, pat_sem, own, tile_a, tile_b, lhs, *rest):
     rows, cols, n_row, n_col = sizes
     panels, rest = rest[:rows], rest[rows:]
     raw, rest = rest[:rows], rest[rows:]
-    raw_sem, z_send, z_recv, x_send, x_recv, fwd_send, keep_sem = rest
+    raw_sem, z_send, z_recv, share_send, x_send, x_recv, fwd_send, keep_sem = rest
     tiles = (tile_a, tile_b)
     zero_at = rows * SLOTS
     chips = n_row // CORES
@@ -30,6 +30,10 @@
     source = [w // ratio for w in wanted]
     shift = [(w % ratio) * rows for w in wanted]
 
+    is_source = [row == source[t] for t in range(2)]
+    is_sibling = [sibling == source[t] for t in range(2)]
+    is_far = [chip != source[t] // CORES for t in range(2)]
+
     barrier = pltpu.get_barrier_semaphore()
     for step in range(1, n_row):
         pl.semaphore_signal(barrier, inc=1, device_id={"row": (row + step) % n_row})
@@ -39,6 +43,8 @@
     def fetch(r):
         return pltpu.make_async_copy(dens.at[pl.ds(r * BLK, BLK)], raw[r], raw_sem.at[r])
 
+    blocks = pltpu.make_async_copy(pat_hbm, pat, pat_sem)
+    blocks.start()
     for r in range(rows):
         fetch(r).start()
 
@@ -69,11 +75,16 @@
             device_id={"col": below},
         )
 
-    def spread(t, r, j):
-        target = sibling if j == 0 else ((chip + j) % chips) * CORES + core
-        return pltpu.make_async_remote_copy(
-            piece(own, r), piece(tiles[t], r), x_send.at[t, r, j], x_recv.at[t, r],
-            device_id={"row": target},
+    def share(t, r):
+        return pltpu.make_async_remote_copy(
+            piece(own, r), piece(tiles[t], r), share_send.at[t, r], x_recv.at[t, r],
+            device_id={"row": sibling},
+        )
+
+    def spread(t, r, j, held):
+        return pltpu.make_async_remote_copy(
+            piece(held, r), piece(tiles[t], r), x_send.at[t, r, j - 1], x_recv.at[t, r],
+            device_id={"row": ((chip + j) % chips) * CORES + core},
         )
 
     def forward(t, r):
@@ -86,6 +97,7 @@
         return pltpu.make_async_copy(piece(own, r), piece(tiles[t], r), keep_sem.at[t, r])
 
     zero = jnp.zeros((BLK, BLK), own.dtype)
+    blocks.wait()
     for r in range(rows):
         fetch(r).wait()
         for s in range(SLOTS):
@@ -98,12 +110,33 @@
         if r == 0:
             pl.semaphore_wait(barrier, n_row + 1)
         down(r).start()
-        for t in range(2):
-            @pl.when(row == source[t])
-            def _():
-                for j in reversed(range(chips)):
-                    spread(t, r, j).start()
+        for t in (1, 0):
+            @pl.when(is_source[t])
+            def _():
+                share(t, r).start()
                 keep(t, r).start()
+
+        @pl.when(is_source[1] & (core == r % CORES))
+        def _():
+            for j in range(1, chips):
+                spread(1, r, j, own).start()
+
+    for t in (1, 0):
+        for r in range(rows):
+            @pl.when(is_sibling[t])
+            def _():
+                share(t, r).wait_recv()
+
+            @pl.when(is_sibling[t] & (core == r % CORES))
+            def _():
+                for j in range(1, chips):
+                    spread(t, r, j, tiles[t]).start()
+
+            if t == 0:
+                @pl.when(is_source[0] & (core == r % CORES))
+                def _():
+                    for j in range(1, chips):
+                        spread(0, r, j, own).start()
 
     own[zero_at] = zero
     tile_b[zero_at] = zero
@@ -115,62 +148,85 @@
         slots = [slot_of(col * rows + k, row, c) for c in range(cols)]
         held.append([jnp.where(slot >= 0, k * SLOTS + slot, zero_at) for slot in slots])
 
-    relays = [(chip != source[t] // CORES) & (core == source[t] % CORES) for t in range(2)]
-    for r in range(rows):
-        for t in range(2):
-            @pl.when(row == source[t])
-            def _():
-                keep(t, r).wait()
-
-            @pl.when(row != source[t])
-            def _():
-                spread(t, r, 0).wait_recv()
-
-            @pl.when(relays[t])
-            def _():
-                forward(t, r).start()
-
-        for c in range(cols):
-            total = None
-            for s in range(SLOTS):
-                column, found = column_of(col * rows + r, source[0], s)
+    def relay(t, r):
+        @pl.when(is_far[t] & (core == r % CORES))
+        def _():
+            forward(t, r).wait_recv()
+            forward(t, r).start()
+
+    def arrive(t, r):
+        @pl.when(is_far[t] & (core != r % CORES))
+        def _():
+            forward(t, r).wait_recv()
+
+        @pl.when(is_source[t])
+        def _():
+            keep(t, r).wait()
+
+    def first_term(r):
+        places = [column_of(col * rows + r, source[0], s) for s in range(SLOTS)]
+        for c in range(cols):
+            where = pl.ds(c * BLK, BLK)
+            total = out[pl.ds(r * BLK, BLK), where]
+            for s, (column, found) in enumerate(places):
                 at = zero_at
                 for k in range(rows):
                     here = (found != 0) & (column == shift[0] + k)
                     at = jnp.where(here, held[k][c], at)
-                term = jnp.dot(
+                total = total + jnp.dot(
                     tile_a[r * SLOTS + s], own[at], preferred_element_type=jnp.float32
                 )
-                total = term if total is None else total + term
-            out[pl.ds(r * BLK, BLK), pl.ds(c * BLK, BLK)] = total
-
-    for k in range(rows):
+            out[pl.ds(r * BLK, BLK), where] = total
+
+    def second_term(k):
         for r in range(rows):
             slot = slot_of(col * rows + r, source[1], shift[1] + k)
             at = jnp.where(slot >= 0, r * SLOTS + slot, zero_at)
             lhs[pl.ds(r * BLK, BLK), :] = tile_b[at]
+        ats = []
+        for c in range(cols):
+            slot = slot_of(above * rows + k, row, c)
+            ats.append(jnp.where(slot >= 0, slot, SLOTS))
         down(k).wait_recv()
-
-        def second_term(c, carry):
-            slot = slot_of(above * rows + k, row, c)
-            at = jnp.where(slot >= 0, slot, SLOTS)
-            where = pl.ds(pl.multiple_of(c * BLK, BLK), BLK)
-            out[:, where] += jnp.dot(
-                lhs[...], panels[k][at], preferred_element_type=jnp.float32
-            )
-            return carry
-
-        lax.fori_loop(0, cols, second_term, 0)
+        for c, at in enumerate(ats):
+            where = pl.ds(c * BLK, BLK)
+            term = jnp.dot(lhs[...], panels[k][at], preferred_element_type=jnp.float32)
+            out[:, where] = term if k == 0 else out[:, where] + term
+
+    half = rows // 2
+    for r in range(rows):
+        relay(1, r)
+    for r in range(rows):
+        arrive(1, r)
+    for k in range(half):
+        second_term(k)
+    for r in range(half):
+        relay(0, r)
+    for r in range(half):
+        arrive(0, r)
+        first_term(r)
+    for k in range(half, rows):
+        if k == rows - 1:
+            for r in range(half, rows):
+                relay(0, r)
+        second_term(k)
+    for r in range(half, rows):
+        arrive(0, r)
+        first_term(r)
 
     for r in range(rows):
         down(r).wait_send()
         for t in range(2):
-            @pl.when(row == source[t])
-            def _():
-                for j in range(chips):
-                    spread(t, r, j).wait_send()
-
-            @pl.when(relays[t])
+            @pl.when(is_source[t])
+            def _():
+                share(t, r).wait_send()
+
+            @pl.when(jnp.logical_not(is_far[t]) & (core == r % CORES))
+            def _():
+                for j in range(1, chips):
+                    spread(t, r, j, own).wait_send()
+
+            @pl.when(is_far[t] & (core == r % CORES))
             def _():
                 forward(t, r).wait_send()
 
@@ -186,11 +242,12 @@
         functools.partial(kernel, (rows, cols, n_row, n_col)),
         out_shape=jax.ShapeDtypeStruct((stripe, width), jnp.float32),
         in_specs=[
-            pl.BlockSpec(memory_space=pltpu.SMEM),
-            pl.BlockSpec(memory_space=pl.ANY),
+            pl.BlockSpec(memory_space=pltpu.HBM),
+            pl.BlockSpec(memory_space=pltpu.HBM),
         ],
         out_specs=pl.BlockSpec(memory_space=pltpu.VMEM),
-        scratch_shapes=[packed] * 3
+        scratch_shapes=[pltpu.SMEM(pattern.shape, pattern.dtype), pltpu.SemaphoreType.DMA]
+        + [packed] * 3
         + [pltpu.VMEM((stripe, BLK), dtype)]
         + [pltpu.VMEM((SLOTS + 1, BLK, BLK), dtype)] * rows
         + [pltpu.VMEM((BLK, width), dtype)] * rows
@@ -198,7 +255,8 @@
             pltpu.SemaphoreType.DMA((rows,)),
             pltpu.SemaphoreType.DMA((rows,)),
             pltpu.SemaphoreType.DMA((rows,)),
-            pltpu.SemaphoreType.DMA((2, rows, chips)),
+            pltpu.SemaphoreType.DMA((2, rows)),
+            pltpu.SemaphoreType.DMA((2, rows, max(chips - 1, 1))),
             pltpu.SemaphoreType.DMA((2, rows)),
             pltpu.SemaphoreType.DMA((2, rows)),
             pltpu.SemaphoreType.DMA((2, rows)),

time: 40.9 us -> 34.8 us (0.85)
  the two profiles are of different devices: /device:TPU:2 before, /device:TPU:0 now
where the time goes in v2:
time: 34.8 us; the launch traced here: 34.3 us
  Pallas kernels  30 us (86%)
  local copies, waits for them, and re-layouts  4.3 us (12%)
    pallas_call x1, Pallas kernels, local(): pl.pallas_call(functools.partial(kernel, (rows, cols, n_row, n_col)), out...  30 us
    unnamed x5, local copies, waits for them, and re-layouts  4.3 us

profile of v2, /device:TPU:0, one launch (start us, length us, event | category | flops | bytes accessed | tf_op | source)
XLA Modules:
  0.0 34.3 jit_solution(8600092423822373966)
XLA Ops:
  0.0 0.0 copy-start
  0.0 1.6 %copy-done = bf16[1024,1024]{1,0:T(8,128)(2,1)S(1)} copy-done((bf16[1024,1024]{1,0:T(8,128)(2,1)S(1)}, bf16[1024,1024]{1,0:T(8,128)(2,1)}, u32[]{:S(2)}) %copy-start) | copy-done | bytes 2097176
  1.6 0.0 copy-start.1
  1.6 0.7 %copy-done.1 = s32[16,16]{1,0:T(8,128)S(1)} copy-done((s32[16,16]{1,0:T(8,128)S(1)}, s32[16,16]{1,0:T(8,128)}, u32[]{:S(2)}) %copy-start.1) | copy-done | bytes 1048
  2.3 30.0 %shard_map.28 = f32[1024,1024]{1,0:T(8,128)S(1)} custom-call(s32[16,16]{1,0:T(8,128)S(1)} %copy-done.1, bf16[1024,1024]{1,0:T(8,128)(2,1)S(1)} %copy-done), custom_call_target="tpu_custom_call" | custom-call | flops 4294967296 | bytes 6291456 | tf_op jit(solution)/shard_map/pallas_call | solution.py:241
  32.3 2.0 %copy.4 = f32[1024,1024]{1,0:T(8,128)} copy(f32[1024,1024]{1,0:T(8,128)S(1)} %shard_map.28) | data formatting | bytes 8388608
Async XLA Ops:
  0.0 1.6 %copy-start = (bf16[1024,1024]{1,0:T(8,128)(2,1)S(1)}, bf16[1024,1024]{1,0:T(8,128)(2,1)}, u32[]{:S(2)}) copy-start(bf16[1024,1024]{1,0:T(8,128)(2,1)} %dens.1) | copy-start | bytes 6291460
  1.6 0.7 %copy-start.1 = (s32[16,16]{1,0:T(8,128)S(1)}, s32[16,16]{1,0:T(8,128)}, u32[]{:S(2)}) copy-start(s32[16,16]{1,0:T(8,128)} %pat_hbm.1) | copy-start | bytes 3076

commit v3 on v2

--- a/solution.py
+++ b/solution.py
@@ -269,7 +269,10 @@
             bytes_accessed=6 * stripe * width,
             transcendentals=0,
         ),
-    )(pattern, density)
+    )(
+        pltpu.with_memory_space_constraint(pattern, pltpu.HBM),
+        pltpu.with_memory_space_constraint(density, pltpu.HBM),
+    )
 
 
 def solution(mesh):

time: 34.8 us -> 32.5 us (0.934)
  local copies, waits for them, and re-layouts: 4.3 us -> 2.02 us
    unnamed x5 -> x1, local copies, waits for them, and re-layouts: 4.3 us -> 2.02 us
where the time goes in v3:
time: 32.5 us; the launch traced here: 32 us
  Pallas kernels  30 us (92%)
  local copies, waits for them, and re-layouts  2.02 us (6%)
    pallas_call x1, Pallas kernels, local(): pl.pallas_call(functools.partial(kernel, (rows, cols, n_row, n_col)), out...  30 us
    unnamed x1, local copies, waits for them, and re-layouts  2.02 us

profile of v3, /device:TPU:0, one launch (start us, length us, event | category | flops | bytes accessed | tf_op | source)
XLA Modules:
  0.0 32.0 jit_solution(16528669963698943082)
XLA Ops:
  0.0 30.0 %shard_map.28 = f32[1024,1024]{1,0:T(8,128)S(1)} custom-call(s32[16,16]{1,0:T(8,128)} %pat_hbm.1, bf16[1024,1024]{1,0:T(8,128)(2,1)} %dens.1), custom_call_target="tpu_custom_call" | custom-call | flops 4294967296 | bytes 6291456 | tf_op jit(solution)/shard_map/pallas_call | solution.py:241
  30.0 2.0 %copy.4 = f32[1024,1024]{1,0:T(8,128)} copy(f32[1024,1024]{1,0:T(8,128)S(1)} %shard_map.28) | data formatting | bytes 8388608

commit v4 on v3

--- a/solution.py
+++ b/solution.py
@@ -12,7 +12,74 @@
 CORES = 2
 
 
-def kernel(sizes, pat_hbm, dens, out, pat, pat_sem, own, tile_a, tile_b, lhs, *rest):
+def find_column(pat, cols, block_row, device, slot):
+    count, column, found = 0, 0, 0
+    for c in range(cols):
+        here = pat[block_row, device * cols + c]
+        hit = jnp.where(count == slot, here, 0)
+        column = column + hit * c
+        found = found + hit
+        count = count + here
+    return column, found
+
+
+def find_slot(pat, cols, block_row, device, column):
+    count, here = 0, 0
+    for c in range(cols):
+        value = pat[block_row, device * cols + c]
+        count = count + jnp.where(c < column, value, 0)
+        here = here + jnp.where(c == column, value, 0)
+    return jnp.where(here == 0, -1, jnp.minimum(count, SLOTS - 1))
+
+
+def held_at(pat, rows, cols, row, col):
+    held = []
+    for k in range(rows):
+        slots = [find_slot(pat, cols, col * rows + k, row, c) for c in range(cols)]
+        held.append([jnp.where(slot >= 0, k * SLOTS + slot, rows * SLOTS) for slot in slots])
+    return held
+
+
+def first_block(places, held, tile_a, own, shift, rows, r, c):
+    total = None
+    for s, (column, found) in enumerate(places):
+        at = rows * SLOTS
+        for k in range(rows):
+            here = (found != 0) & (column == shift + k)
+            at = jnp.where(here, held[k][c], at)
+        term = jnp.dot(tile_a[r * SLOTS + s], own[at], preferred_element_type=jnp.float32)
+        total = term if total is None else total + term
+    return total
+
+
+def finish(sizes, pat_hbm, total, own, tile_a, out, pat, pat_sem, last, sems):
+    rows, cols = sizes
+    half = rows // 2
+    row, col = lax.axis_index("row"), lax.axis_index("col")
+    ratio = cols // rows
+    blocks = pltpu.make_async_copy(pat_hbm, pat, pat_sem)
+    blocks.start()
+
+    def write(r):
+        ready = total.at[pl.ds(r * BLK, BLK)] if r < half else last.at[r - half]
+        return pltpu.make_async_copy(ready, out.at[pl.ds(r * BLK, BLK)], sems.at[r])
+
+    for r in range(half):
+        write(r).start()
+    blocks.wait()
+    held = held_at(pat, rows, cols, row, col)
+    for r in range(half, rows):
+        places = [find_column(pat, cols, col * rows + r, col // ratio, s) for s in range(SLOTS)]
+        for c in range(cols):
+            where = pl.ds(c * BLK, BLK)
+            block = first_block(places, held, tile_a, own, (col % ratio) * rows, rows, r, c)
+            last[r - half, :, where] = total[pl.ds(r * BLK, BLK), where] + block
+        write(r).start()
+    for r in range(rows):
+        write(r).wait()
+
+
+def kernel(sizes, pat_hbm, dens, out, own, tile_a, pat, pat_sem, tile_b, lhs, *rest):
     rows, cols, n_row, n_col = sizes
     panels, rest = rest[:rows], rest[rows:]
     raw, rest = rest[:rows], rest[rows:]
@@ -40,6 +107,9 @@
     pl.semaphore_signal(barrier, inc=1, device_id={"col": below})
     pl.semaphore_signal(barrier, inc=1, device_id={"col": above})
 
+    def turn(t, r):
+        return core == (source[t] + r) % CORES
+
     def fetch(r):
         return pltpu.make_async_copy(dens.at[pl.ds(r * BLK, BLK)], raw[r], raw_sem.at[r])
 
@@ -48,23 +118,8 @@
     for r in range(rows):
         fetch(r).start()
 
-    def column_of(block_row, device, slot):
-        count, column, found = 0, 0, 0
-        for c in range(cols):
-            here = pat[block_row, device * cols + c]
-            hit = jnp.where(count == slot, here, 0)
-            column = column + hit * c
-            found = found + hit
-            count = count + here
-        return column, found
-
-    def slot_of(block_row, device, column):
-        count, here = 0, 0
-        for c in range(cols):
-            value = pat[block_row, device * cols + c]
-            count = count + jnp.where(c < column, value, 0)
-            here = here + jnp.where(c == column, value, 0)
-        return jnp.where(here == 0, -1, jnp.minimum(count, SLOTS - 1))
+    column_of = functools.partial(find_column, pat, cols)
+    slot_of = functools.partial(find_slot, pat, cols)
 
     def piece(ref, r):
         return ref.at[pl.ds(r * SLOTS, SLOTS)]
@@ -109,6 +164,11 @@
             own[r * SLOTS + s] = block
         if r == 0:
             pl.semaphore_wait(barrier, n_row + 1)
+        @pl.when(is_source[1] & turn(1, r))
+        def _():
+            for j in range(1, chips):
+                spread(1, r, j, own).start()
+
         down(r).start()
         for t in (1, 0):
             @pl.when(is_source[t])
@@ -116,24 +176,19 @@
                 share(t, r).start()
                 keep(t, r).start()
 
-        @pl.when(is_source[1] & (core == r % CORES))
-        def _():
-            for j in range(1, chips):
-                spread(1, r, j, own).start()
-
     for t in (1, 0):
         for r in range(rows):
             @pl.when(is_sibling[t])
             def _():
                 share(t, r).wait_recv()
 
-            @pl.when(is_sibling[t] & (core == r % CORES))
+            @pl.when(is_sibling[t] & turn(t, r))
             def _():
                 for j in range(1, chips):
                     spread(t, r, j, tiles[t]).start()
 
             if t == 0:
-                @pl.when(is_source[0] & (core == r % CORES))
+                @pl.when(is_source[0] & turn(0, r))
                 def _():
                     for j in range(1, chips):
                         spread(0, r, j, own).start()
@@ -143,19 +198,16 @@
     for r in range(rows):
         panels[r][SLOTS] = zero
 
-    held = []
-    for k in range(rows):
-        slots = [slot_of(col * rows + k, row, c) for c in range(cols)]
-        held.append([jnp.where(slot >= 0, k * SLOTS + slot, zero_at) for slot in slots])
+    held = held_at(pat, rows, cols, row, col)
 
     def relay(t, r):
-        @pl.when(is_far[t] & (core == r % CORES))
+        @pl.when(is_far[t] & turn(t, r))
         def _():
             forward(t, r).wait_recv()
             forward(t, r).start()
 
     def arrive(t, r):
-        @pl.when(is_far[t] & (core != r % CORES))
+        @pl.when(is_far[t] & jnp.logical_not(turn(t, r)))
         def _():
             forward(t, r).wait_recv()
 
@@ -167,16 +219,9 @@
         places = [column_of(col * rows + r, source[0], s) for s in range(SLOTS)]
         for c in range(cols):
             where = pl.ds(c * BLK, BLK)
-            total = out[pl.ds(r * BLK, BLK), where]
-            for s, (column, found) in enumerate(places):
-                at = zero_at
-                for k in range(rows):
-                    here = (found != 0) & (column == shift[0] + k)
-                    at = jnp.where(here, held[k][c], at)
-                total = total + jnp.dot(
-                    tile_a[r * SLOTS + s], own[at], preferred_element_type=jnp.float32
-                )
-            out[pl.ds(r * BLK, BLK), where] = total
+            out[pl.ds(r * BLK, BLK), where] += first_block(
+                places, held, tile_a, own, shift[0], rows, r, c
+            )
 
     def second_term(k):
         for r in range(rows):
@@ -212,7 +257,6 @@
         second_term(k)
     for r in range(half, rows):
         arrive(0, r)
-        first_term(r)
 
     for r in range(rows):
         down(r).wait_send()
@@ -221,12 +265,12 @@
             def _():
                 share(t, r).wait_send()
 
-            @pl.when(jnp.logical_not(is_far[t]) & (core == r % CORES))
+            @pl.when(jnp.logical_not(is_far[t]) & turn(t, r))
             def _():
                 for j in range(1, chips):
                     spread(t, r, j, own).wait_send()
 
-            @pl.when(is_far[t] & (core == r % CORES))
+            @pl.when(is_far[t] & turn(t, r))
             def _():
                 forward(t, r).wait_send()
 
@@ -238,16 +282,19 @@
     chips = n_row // CORES
     dtype = density.dtype
     packed = pltpu.VMEM((rows * SLOTS + 1, BLK, BLK), dtype)
-    return pl.pallas_call(
+    kept = jax.ShapeDtypeStruct((rows * SLOTS + 1, BLK, BLK), dtype)
+    result = jax.ShapeDtypeStruct((stripe, width), jnp.float32)
+    pattern = pltpu.with_memory_space_constraint(pattern, pltpu.HBM)
+    total, own, tile_a = pl.pallas_call(
         functools.partial(kernel, (rows, cols, n_row, n_col)),
-        out_shape=jax.ShapeDtypeStruct((stripe, width), jnp.float32),
+        out_shape=(result, kept, kept),
         in_specs=[
             pl.BlockSpec(memory_space=pltpu.HBM),
             pl.BlockSpec(memory_space=pltpu.HBM),
         ],
-        out_specs=pl.BlockSpec(memory_space=pltpu.VMEM),
+        out_specs=[pl.BlockSpec(memory_space=pltpu.VMEM)] * 3,
         scratch_shapes=[pltpu.SMEM(pattern.shape, pattern.dtype), pltpu.SemaphoreType.DMA]
-        + [packed] * 3
+        + [packed]
         + [pltpu.VMEM((stripe, BLK), dtype)]
         + [pltpu.VMEM((SLOTS + 1, BLK, BLK), dtype)] * rows
         + [pltpu.VMEM((BLK, width), dtype)] * rows
@@ -270,9 +317,24 @@
             transcendentals=0,
         ),
     )(
-        pltpu.with_memory_space_constraint(pattern, pltpu.HBM),
+        pattern,
         pltpu.with_memory_space_constraint(density, pltpu.HBM),
     )
+    keep = [pltpu.with_memory_space_constraint(x, pltpu.VMEM) for x in (total, own, tile_a)]
+    return pl.pallas_call(
+        functools.partial(finish, (rows, cols)),
+        out_shape=result,
+        in_specs=[pl.BlockSpec(memory_space=pltpu.HBM)]
+        + [pl.BlockSpec(memory_space=pltpu.VMEM)] * 3,
+        out_specs=pl.BlockSpec(memory_space=pltpu.HBM),
+        scratch_shapes=[
+            pltpu.SMEM(pattern.shape, pattern.dtype),
+            pltpu.SemaphoreType.DMA,
+            pltpu.VMEM((rows - rows // 2, BLK, width), jnp.float32),
+            pltpu.SemaphoreType.DMA((rows,)),
+        ],
+        compiler_params=pltpu.CompilerParams(vmem_limit_bytes=24 * 1024 * 1024),
+    )(pattern, *keep)
 
 
 def solution(mesh):

time: 32.5 us -> 32.1 us (0.988)
  local copies, waits for them, and re-layouts: 2.02 us -> 0 us
  Pallas kernels: 30 us -> 31.9 us
    pallas_call x0 -> x1, Pallas kernels: none -> 2.64 us  [local(): pl.pallas_call(functools.partial(finish, (rows, cols)), out_shape=result,...]
    unnamed x1 -> x0, local copies, waits for them, and re-layouts: 2.02 us -> none
    pallas_call x1, Pallas kernels: 30 us -> 29.2 us  [local(): pl.pallas_call(functools.partial(kernel, (rows, cols, n_row, n_col)), out...]
where the time goes in v4:
time: 32.1 us; the launch traced here: 31.9 us
  Pallas kernels  31.9 us (99%)
    pallas_call x1, Pallas kernels, local(): pl.pallas_call(functools.partial(kernel, (rows, cols, n_row, n_col)), out...  29.2 us
    pallas_call x1, Pallas kernels, local(): pl.pallas_call(functools.partial(finish, (rows, cols)), out_shape=result,...  2.64 us

profile of v4, /device:TPU:0, one launch (start us, length us, event | category | flops | bytes accessed | tf_op | source)
XLA Modules:
  0.0 31.9 jit_solution(4338854083445668254)
XLA Ops:
  0.0 29.2 %shard_map.28 = (f32[1024,1024]{1,0:T(8,128)S(1)}, bf16[9,256,256]{2,1,0:T(8,128)(2,1)S(1)}, bf16[9,256,256]{2,1,0:T(8,128)(2,1)S(1)}) custom-call(s32[16,16]{1,0:T(8,128)} %pat_hbm.3, bf16[1024,1024]{1,0:T(8,128)(2,1)} %dens.1), custom_call_target="tpu_custom_call" | custom-call | flops 4294967296 | bytes 6291456 | tf_op jit(solution)/shard_map/pallas_call | solution.py:288
  29.2 2.6 %shard_map.29 = f32[1024,1024]{1,0:T(8,128)} custom-call(s32[16,16]{1,0:T(8,128)} %pat_hbm.3, f32[1024,1024]{1,0:T(8,128)S(1)} %get-tuple-element.8.total, bf16[9,256,256]{2,1,0:T(8,128)(2,1)S(1)} %get-tuple-element.9.own, bf16[9,256,256]{2,1,0:T(8,128)(2,1)S(1)} %get-tuple-element.10.tile_a), custom_call_target="tpu_custom_call" | custom-call | tf_op jit(solution)/shard_map/pallas_call | solution.py:324
